TPU v7x, 32 devices: a whole 2x2x4 slice. The times are simulated.
32 devices in a mesh: mesh: 4 (over y, core), mode: 8 (over z, x).
Axes of the slice: x: 2, y: 2, z: 4, core: 2. Of those that a mesh axis runs over, the one named last changes fastest.
Arguments:
- field: float32 [256, 512, 1024], P('mode', 'mesh'), may hold values from -6 to 6
- kappa: bfloat16 [3, 512, 1024], P(None, ('mesh', 'mode')), may hold values from 0.099609375 to 1
- mass: float32 [512, 1024], P(('mesh', 'mode')), may hold values from 0.5 to 1.5
- kl_modes: bfloat16 [3, 256, 256], replicated, may hold values from -0.375 to 0.375
- to_points: bfloat16 [512, 256], replicated, may hold values from -0.375 to 0.375
- from_points: bfloat16 [256, 512], replicated, may hold values from -0.25 to 0.25
- capacity: float32 [512], replicated, may hold values from 0.5 to 2
- latent: float32 [512], replicated, may hold values from 0.5 to 3
Outputs:
- residual: bfloat16 [256, 512, 1024], P('mode', 'mesh')
All inputs are finite; a program needn't handle non-finite values.
Results may differ from a plain program's by a relative error of at most 0.0058.
Values may be sent and summed in bfloat16 or wider, within the bound.
A program may use at most 256 MiB of HBM per device.

v0:
```python
import jax
import jax.numpy as jnp
from jax import lax
from jax.sharding import PartitionSpec as P


def extended(cells, sides, width):
    for axis, dim in sides:
        count = lax.axis_size(axis)
        ends = count - 1
        head = lax.slice_in_dim(cells, 0, width, axis=dim)
        tail = lax.slice_in_dim(cells, cells.shape[dim] - width, cells.shape[dim], axis=dim)
        cells = jnp.concatenate(
            [
                lax.ppermute(tail, axis, [(i, (i + 1) % count) for i in range(ends)]),
                cells,
                lax.ppermute(head, axis, [((i + 1) % count, i) for i in range(ends)]),
            ],
            axis=dim,
        )
    return cells


def conduct(values, kappa):
    count = values.shape[1] - 2
    width = values.shape[2]
    vals = jnp.pad(values.astype(jnp.float32), ((0, 0), (0, 0), (1, 1)))[None]
    kaps = jnp.pad(kappa.astype(jnp.float32), ((0, 0), (0, 0), (1, 1)))[:, None]
    centre = vals[:, :, 1 : 1 + count, 1 : 1 + width]
    kcentre = kaps[:, :, 1 : 1 + count, 1 : 1 + width]
    total = jnp.zeros((kaps.shape[0], vals.shape[1], count, width), jnp.float32)
    for shift_x, shift_y in ((0, 1), (2, 1), (1, 0), (1, 2)):
        other = vals[:, :, shift_x : shift_x + count, shift_y : shift_y + width]
        kother = kaps[:, :, shift_x : shift_x + count, shift_y : shift_y + width]
        total = total + 0.5 * (kcentre + kother) * (centre - other)
    return total.astype(jnp.bfloat16)


def finish(coarse, images, mass_rows, kl_modes, to_points, from_points, capacity, latent):
    mixed = jnp.einsum("kij,kjxy->ixy", kl_modes, images, preferred_element_type=jnp.float32)
    temps = jnp.einsum("qi,ixy->qxy", to_points, coarse, preferred_element_type=jnp.float32)
    heat = (
        capacity[:, None, None] * temps + latent[:, None, None] * jax.nn.sigmoid(2.0 * temps)
    ).astype(jnp.bfloat16)
    enthalpy = jnp.einsum("iq,qxy->ixy", from_points, heat, preferred_element_type=jnp.float32)
    return (mass_rows[None] * enthalpy + mixed).astype(jnp.bfloat16)


def body(field, kappa, mass, kl_modes, to_points, from_points, capacity, latent):
    coarse = field.astype(jnp.bfloat16)
    owned = coarse.shape[0]
    width = coarse.shape[2]
    groups = lax.axis_size("mode")
    terms = kappa.shape[0]
    kap_rows = lax.all_gather(kappa, "mode", axis=1, tiled=True)
    stacked = jnp.concatenate([coarse, kap_rows], 0)
    padded = extended(stacked, (("mesh", 1),), 1)
    images = conduct(padded[:owned], padded[owned:])
    joined = jnp.concatenate([coarse[None], images], 0)
    joined = joined.reshape((terms + 1) * owned, coarse.shape[1], width)
    moved = lax.all_to_all(joined, "mode", split_axis=1, concat_axis=0, tiled=True)
    node_rows = moved.shape[1]
    moved = moved.reshape(groups, terms + 1, owned, node_rows, width)
    moved = jnp.transpose(moved, (1, 0, 2, 3, 4)).reshape(
        terms + 1, groups * owned, node_rows, width
    )
    node_coarse = moved[0]
    node_images = moved[1:]
    result = finish(
        node_coarse, node_images, mass, kl_modes, to_points, from_points, capacity, latent
    )
    return lax.all_to_all(result, "mode", split_axis=0, concat_axis=1, tiled=True)


def solution(mesh):
    in_specs = (
        P("mode", "mesh", None),
        P(None, ("mesh", "mode"), None),
        P(("mesh", "mode"), None),
        P(),
        P(),
        P(),
        P(),
        P(),
    )
    out_specs = P("mode", "mesh", None)
    return jax.shard_map(body, mesh=mesh, in_specs=in_specs, out_specs=out_specs, check_vma=False)
```

profile of v0, /device:TPU:1, one launch (start us, length us, event | category | flops | bytes accessed | tf_op | source)
XLA Modules:
  0.0 1315.9 jit_solution(11272950333644281777)
XLA Ops:
  0.0 0.0 copy-start
  0.0 0.0 slice-start
  0.0 0.0 slice-start.1
  0.0 0.0 slice-start.2
  0.0 0.0 copy-start.2
  0.0 16.5 %copy.54 = bf16[32,128,1024]{2,0,1:T(8,128)(2,1)S(1)} copy(f32[32,128,1024]{2,1,0:T(8,128)} %param.8) | data formatting | bytes 25165824 | tf_op args[0]
  16.6 0.0 copy-done.2
  16.6 0.0 copy-start.1
  16.6 28.1 %all_gather.3 = bf16[3,128,1024]{2,1,0:T(8,128)(2,1)S(1)} all-gather(bf16[3,16,1024]{2,1,0:T(8,128)(2,1)S(1)} %copy-done.2), channel_id=1, replica_groups=mesh['mesh'=4,'mode'=8] {'mode'}, dimensions={1}, use_global_device_ids=true | all-gather | bytes 884736 | tf_op jit(solution)/shard_map/all_gather | solution.py:55
  44.6 0.7 copy.32
  45.3 0.0 slice-start.3
  45.4 9.1 collective-permute-start
  54.5 2.1 collective-permute-start.1
  56.7 0.0 slice-done
  56.7 0.0 slice-done.1
  56.7 0.0 slice-done.2
  56.7 0.0 slice-done.3
  56.7 11.4 copy.56
  68.1 0.0 collective-permute-done
  68.1 0.0 collective-permute-done.1
  68.1 0.0 copy-done.1
  68.1 12.0 fusion.11
  80.1 51.1 %fusion.6 = (f32[32,128,1024]{2,0,1:T(8,128)}, f32[32,128,1024]{2,0,1:T(8,128)}, f32[32,128,1024]{2,0,1:T(8,128)}, f32[32,128,1024]{2,0,1:T(8,128)}) fusion(f32[1,32,130,1026]{3,1,2,0:T(8,128)} %fusion.11), kind=kLoop, calls=%fused_computation.15 | loop fusion | flops 16777216 | bytes 150994944 | tf_op jit(solution)/shard_map/mul | solution.py:35
  131.2 0.0 slice-start.4
  131.2 0.0 slice-start.5
  131.2 2.9 fusion.38
  134.1 0.0 slice-start.6
  134.1 0.0 slice-start.7
  134.1 4.5 fusion.36
  138.6 0.0 slice-done.4
  138.6 0.0 slice-done.5
  138.7 0.0 slice-done.6
  138.7 0.0 slice-done.7
  138.7 46.6 %add_convert_fusion = bf16[3,32,128,1024]{3,1,0,2:T(8,128)(2,1)} fusion(f32[32,128,1024]{2,0,1:T(8,128)} %get-tuple-element.8, f32[3,128,1024]{2,0,1:T(4,128)S(1)} %get-tuple-element.14, f32[32,128,1024]{2,0,1:T(8,128)} %get-tuple-element.6, f32[3,128,1024]{2,0,1:T(4,128)S(1)} %get-tuple-element.12, f32[32,128,1024]{2,0,1:T(8,128)} %get-tuple-element.7, ...), kind=kLoop, calls=%fused_computation | loop fusion | flops 100663296 | bytes 98566144 | tf_op jit(solution)/shard_map/convert_element_type | solution.py:36
  185.3 23.1 %pad_maximum_fusion = bf16[4,32,128,1024]{3,1,0,2:T(8,128)(2,1)} fusion(bf16[3,32,128,1024]{3,1,0,2:T(8,128)(2,1)} %add_convert_fusion, bf16[1,32,128,1024]{3,1,0,2:T(8,128)(2,1)} %bitcast.79), kind=kLoop, calls=%fused_computation.1 | loop fusion | flops 16777216 | bytes 67108864 | tf_op jit(solution)/shard_map/concatenate | solution.py:59
  208.4 733.1 %all_to_all.33 = bf16[128,128,1024]{2,0,1:T(8,128)(2,1)} all-to-all(bf16[128,128,1024]{2,0,1:T(8,128)(2,1)} %bitcast.72), channel_id=1, replica_groups=mesh['mesh'=4,'mode'=8] {'mode'}, dimensions={1} | all-to-all | bytes 67108864 | tf_op jit(solution)/shard_map/all_to_all | solution.py:61
  941.5 30.8 %copy.35 = bf16[8,128,16,1024]{3,2,1,0:T(8,128)(2,1)} copy(bf16[8,128,16,1024]{3,1,2,0:T(8,128)(2,1)} %bitcast.73) | data formatting | bytes 67108864 | tf_op jit(solution)/shard_map/all_to_all | solution.py:61
  972.3 21.4 %slice.80 = bf16[3,8,32,16,1024]{4,3,2,0,1:T(8,128)(2,1)} slice(bf16[4,8,32,16,1024]{4,3,2,0,1:T(8,128)(2,1)} %bitcast.70), slice={[1:4], [0:8], [0:32], [0:16], [0:1024]} | slice | bytes 50331648 | tf_op jit(solution)/shard_map/slice | solution.py:68
  993.7 8.7 slice.79
  1002.4 21.3 %copy.37 = bf16[3,8,32,16,1024]{4,3,2,1,0:T(8,128)(2,1)} copy(bf16[3,8,32,16,1024]{4,3,2,0,1:T(8,128)(2,1)} %slice.80) | data formatting | bytes 50331648 | tf_op jit(solution)/shard_map/slice | solution.py:68
  1023.7 0.0 copy-done
  1023.7 0.0 copy-start.3
  1023.7 0.0 copy-start.4
  1023.7 0.0 copy-start.5
  1023.8 0.0 copy-start.6
  1023.8 0.0 copy-start.7
  1023.8 59.9 %fusion = f32[16,1024,256,1]{2,1,3,0:T(8,128)} fusion(bf16[3,256,16,1024]{3,2,1,0:T(8,128)(2,1)} %bitcast.80, bf16[3,256,256]{2,1,0:T(8,128)(2,1)S(1)} %copy-done), kind=kOutput, calls=%fused_computation.5 | convolution fusion | flops 6442450944 | bytes 42336256 | tf_op jit(solution)/shard_map/kij,kjxy->ixy/dot_general | solution.py:40
  1083.7 0.0 copy-done.3
  1083.7 0.0 copy-done.4
  1083.7 0.0 copy-done.5
  1083.8 0.0 copy-done.6
  1083.8 0.0 copy-done.7
  1083.8 22.9 %fusion.23 = bf16[256,16,1024]{0,2,1:T(8,128)(2,1)} fusion(f32[16,1024,256,1]{2,1,3,0:T(8,128)} %fusion, f32[512]{0:T(512)S(1)} %copy-done.6, f32[512]{0:T(512)S(1)} %copy-done.7, bf16[256,16,1024]{2,1,0:T(8,128)(2,1)} %bitcast.81, f32[16,1024]{1,0:T(8,128)S(1)} %copy-done.5, bf16[256,512]{1,0:T(8,128)(2,1)S(1)} %copy-done.3, bf16[512,256]{1,0:T(8,128)(2,1)S(1)} %copy-done.4), kind=kOutput, calls=%fused_computation.30 | convolution fusion | flops 8669626368 | bytes 34148352 | tf_op jit(solution)/shard_map/iq,qxy->ixy/dot_general | solution.py:45
  1106.6 12.2 copy.39
  1118.9 187.9 %all_to_all.34 = bf16[256,16,1024]{2,1,0:T(8,128)(2,1)} all-to-all(bf16[256,16,1024]{2,1,0:T(8,128)(2,1)} %copy.39), channel_id=1, replica_groups=mesh['mesh'=4,'mode'=8] {'mode'}, dimensions={0} | all-to-all | bytes 16777216 | tf_op jit(solution)/shard_map/all_to_all | solution.py:72
  1306.8 8.7 copy.40
  (3 shorter events, 0.0 us)
Async XLA Ops:
  0.0 1023.7 %copy-start = (bf16[3,256,256]{2,1,0:T(8,128)(2,1)S(1)}, bf16[3,256,256]{2,1,0:T(8,128)(2,1)}, u32[]{:S(2)}) copy-start(bf16[3,256,256]{2,1,0:T(8,128)(2,1)} %param.11) | copy-start | bytes 1179652
  0.0 56.6 %slice-start = ((s8[16777216]{0:T(1024)(128)(4,1)}), s8[4194304]{0:T(1024)(128)(4,1)S(1)}, s32[]{:S(2)}) async-start(s8[16777216]{0:T(1024)(128)(4,1)} %bitcast.74), calls=%async_computation.2 | async-start | bytes 8388608
  0.0 56.7 %slice-start.1 = ((s8[16777216]{0:T(1024)(128)(4,1)}), s8[4194304]{0:T(1024)(128)(4,1)S(1)}, s32[]{:S(2)}) async-start(s8[16777216]{0:T(1024)(128)(4,1)} %bitcast.74), calls=%async_computation.3 | async-start | bytes 8388608
  0.0 56.7 %slice-start.2 = ((s8[16777216]{0:T(1024)(128)(4,1)}), s8[4194304]{0:T(1024)(128)(4,1)S(1)}, s32[]{:S(2)}) async-start(s8[16777216]{0:T(1024)(128)(4,1)} %bitcast.74), calls=%async_computation.4 | async-start | bytes 8388608
  0.0 16.6 %copy-start.2 = (bf16[3,16,1024]{2,1,0:T(8,128)(2,1)S(1)}, bf16[3,16,1024]{2,1,0:T(8,128)(2,1)}, u32[]{:S(2)}) copy-start(bf16[3,16,1024]{2,1,0:T(8,128)(2,1)} %param.9) | copy-start | bytes 294916
  16.6 51.5 %copy-start.1 = (bf16[32,128,1024]{2,0,1:T(8,128)(2,1)}, bf16[32,128,1024]{2,0,1:T(8,128)(2,1)S(1)}, u32[]{:S(2)}) copy-start(bf16[32,128,1024]{2,0,1:T(8,128)(2,1)S(1)} %copy.54) | copy-start | bytes 25165828
  45.3 11.4 slice-start.3
  45.4 22.8 %collective-permute-start = (bf16[35,1,1024]{2,0,1:T(8,128)(2,1)S(1)}, bf16[35,1,1024]{2,0,1:T(8,128)(2,1)S(1)}, u32[]{:S(2)}, u32[]{:S(2)}) collective-permute-start(bf16[35,1,1024]{2,0,1:T(8,128)(2,1)S(1)} %get-tuple-element.9), channel_id=1, source_target_pairs={{0,8},{8,16},{16,24},{1,9},{9,17},{17,25},{2,10},{10,18},{18,26},{... | collective-permute-start | bytes 215048 | tf_op jit(solution)/shard_map/ppermute | solution.py:15
  54.5 13.6 %collective-permute-start.1 = (bf16[35,1,1024]{2,0,1:T(8,128)(2,1)S(1)}, bf16[35,1,1024]{2,0,1:T(8,128)(2,1)S(1)}, u32[]{:S(2)}, u32[]{:S(2)}) collective-permute-start(bf16[35,1,1024]{2,0,1:T(8,128)(2,1)S(1)} %get-tuple-element.10), channel_id=1, source_target_pairs={{8,0},{16,8},{24,16},{9,1},{17,9},{25,17},{10,2},{18,10},{26,18},{... | collective-permute-start | bytes 215048 | tf_op jit(solution)/shard_map/ppermute | solution.py:17
  131.2 7.5 slice-start.4
  131.2 7.5 slice-start.5
  134.1 4.6 slice-start.6
  134.1 4.6 slice-start.7
  1023.7 60.0 %copy-start.3 = (bf16[256,512]{1,0:T(8,128)(2,1)S(1)}, bf16[256,512]{1,0:T(8,128)(2,1)}, u32[]{:S(2)}) copy-start(bf16[256,512]{1,0:T(8,128)(2,1)} %param.13) | copy-start | bytes 786436
  1023.7 60.0 %copy-start.4 = (bf16[512,256]{1,0:T(8,128)(2,1)S(1)}, bf16[512,256]{1,0:T(8,128)(2,1)}, u32[]{:S(2)}) copy-start(bf16[512,256]{1,0:T(8,128)(2,1)} %param.12) | copy-start | bytes 786436
  1023.7 60.0 %copy-start.5 = (f32[16,1024]{1,0:T(8,128)S(1)}, f32[16,1024]{1,0:T(8,128)}, u32[]{:S(2)}) copy-start(f32[16,1024]{1,0:T(8,128)} %param.10) | copy-start | bytes 196612
  1023.8 60.0 %copy-start.6 = (f32[512]{0:T(512)S(1)}, f32[512]{0:T(512)}, u32[]{:S(2)}) copy-start(f32[512]{0:T(512)} %param.15) | copy-start | bytes 6148
  1023.8 60.0 %copy-start.7 = (f32[512]{0:T(512)S(1)}, f32[512]{0:T(512)}, u32[]{:S(2)}) copy-start(f32[512]{0:T(512)} %param.14) | copy-start | bytes 6148
where the time goes:
time: 1320 us
  blocking collectives  949 us (72%)
  other arithmetic  140 us (11%)
  local copies, waits for them, and re-layouts  132 us (10%)
  matrix products  82.8 us (6%)
    all_to_all x1, blocking collectives, body(): lax.all_to_all(joined, 'mode', split_axis=1, concat_axis=0, tiled=True)  733 us
    all_to_all x1, blocking collectives, body(): lax.all_to_all(result, 'mode', split_axis=0, concat_axis=1, tiled=True)  188 us
    dot_general x1, matrix products, finish(): jnp.einsum('kij,kjxy->ixy', kl_modes, images, preferred_element_type=jnp....  59.9 us
    mul x2, other arithmetic, conduct(): total = total + 0.5 * (kcentre + kother) * (centre - other)  55.6 us
    convert_element_type x1, other arithmetic, conduct(): return total.astype(jnp.bfloat16)  46.6 us
    slice x2, local copies, waits for them, and re-layouts, body(): node_images = moved[1:]  42.7 us
    all_to_all x1, local copies, waits for them, and re-layouts, body(): lax.all_to_all(joined, 'mode', split_axis=1, concat_axis=0, tiled=True)  30.8 us
    all_gather x1, blocking collectives, body(): kap_rows = lax.all_gather(kappa, 'mode', axis=1, tiled=True)  28.1 us
  transfers between devices with their start and end apart: 2, of which 0 were waited for; matrix products, arithmetic and copies ran while one was open for 1% of the time, Pallas kernels for 0%

commit v1 on v0

--- a/solution.py
+++ b/solution.py
@@ -2,6 +2,29 @@
 import jax.numpy as jnp
 from jax import lax
 from jax.sharding import PartitionSpec as P
+
+
+def in_blocks(x, dim, size):
+    shape = x.shape
+    blocks = x.reshape(*shape[:dim], size, shape[dim] // size, *shape[dim + 1 :])
+    return jnp.moveaxis(blocks, dim, 0)
+
+
+def laid_out(parts, dim):
+    shape = list(parts.shape[1:])
+    shape[dim] *= parts.shape[0]
+    return jnp.moveaxis(parts, 0, dim).reshape(shape)
+
+
+def sent_to_each(x, axis, split_dim, concat_dim):
+    size, position = (lax.axis_size(axis), lax.axis_index(axis))
+    pieces = in_blocks(x, split_dim, size)
+    gathered = [pieces[position]]
+    for step in range(1, size):
+        sent = pieces[(position + step) % size]
+        gathered.append(lax.ppermute(sent, axis, [(i, (i + step) % size) for i in range(size)]))
+    pieces = jnp.stack(gathered)[(position - jnp.arange(size)) % size]
+    return laid_out(pieces, concat_dim)
 
 
 def extended(cells, sides, width):
@@ -58,7 +81,7 @@
     images = conduct(padded[:owned], padded[owned:])
     joined = jnp.concatenate([coarse[None], images], 0)
     joined = joined.reshape((terms + 1) * owned, coarse.shape[1], width)
-    moved = lax.all_to_all(joined, "mode", split_axis=1, concat_axis=0, tiled=True)
+    moved = sent_to_each(joined, "mode", 1, 0)
     node_rows = moved.shape[1]
     moved = moved.reshape(groups, terms + 1, owned, node_rows, width)
     moved = jnp.transpose(moved, (1, 0, 2, 3, 4)).reshape(

time: 1320 us -> 1500 us (1.14)
  blocking collectives: 949 us -> 409 us
  waiting for transfers between devices: 0.01 us -> 408 us
  local copies, waits for them, and re-layouts: 132 us -> 313 us
  starting transfers between devices: 11.3 us -> 109 us
  matrix products: 82.8 us -> 101 us
    all_to_all x1 -> x0, blocking collectives: 733 us -> none  [body(): lax.all_to_all(joined, 'mode', split_axis=1, concat_axis=0, tiled=True)]
    ppermute x0 -> x7, waiting for transfers between devices: none -> 408 us  [sent_to_each(): lax.ppermute(sent, axis, [(i, (i + step) % size) for i in range(size)])]
    all_to_all x1, blocking collectives: 188 us -> 381 us  [body(): lax.all_to_all(result, 'mode', split_axis=0, concat_axis=1, tiled=True)]
    ppermute x0 -> x7, starting transfers between devices: none -> 97.6 us  [sent_to_each(): lax.ppermute(sent, axis, [(i, (i + step) % size) for i in range(size)])]
    mul x0 -> x8, local copies, waits for them, and re-layouts: none -> 82.9 us  [conduct(): total = total + 0.5 * (kcentre + kother) * (centre - other)]
    gather x0 -> x5, local copies, waits for them, and re-layouts: none -> 56.5 us  [sent_to_each(): pieces = jnp.stack(gathered)[(position - jnp.arange(size)) % size]]
    unnamed x34 -> x57, local copies, waits for them, and re-layouts: 28 us -> 63.4 us
    all_to_all x1 -> x0, local copies, waits for them, and re-layouts: 30.8 us -> none  [body(): lax.all_to_all(joined, 'mode', split_axis=1, concat_axis=0, tiled=True)]
  transfers between devices with their start and end apart: 2 -> 9, of which waited for: 0 -> 4; matrix products, arithmetic and copies ran while one was open for 1% -> 4% of each run, Pallas kernels for 0% -> 0%
where the time goes in v1:
time: 1500 us; the launch traced here: 1490 us
  blocking collectives  409 us (27%)
  waiting for transfers between devices  408 us (27%)
  local copies, waits for them, and re-layouts  313 us (21%)
  other arithmetic  150 us (10%)
  starting transfers between devices  109 us (7%)
  matrix products  101 us (7%)
    ppermute x7, waiting for transfers between devices, sent_to_each(): lax.ppermute(sent, axis, [(i, (i + step) % size) for i in range(size)])  408 us
    all_to_all x1, blocking collectives, body(): lax.all_to_all(result, 'mode', split_axis=0, concat_axis=1, tiled=True)  381 us
    ppermute x7, starting transfers between devices, sent_to_each(): lax.ppermute(sent, axis, [(i, (i + step) % size) for i in range(size)])  97.6 us
    mul x8, local copies, waits for them, and re-layouts, conduct(): total = total + 0.5 * (kcentre + kother) * (centre - other)  82.9 us
    dot_general x1, matrix products, finish(): jnp.einsum('kij,kjxy->ixy', kl_modes, images, preferred_element_type=jnp....  77.9 us
    unnamed x57, local copies, waits for them, and re-layouts  63.4 us
    gather x5, local copies, waits for them, and re-layouts, sent_to_each(): pieces = jnp.stack(gathered)[(position - jnp.arange(size)) % size]  56.5 us
    mul x2, other arithmetic, conduct(): total = total + 0.5 * (kcentre + kother) * (centre - other)  56.1 us
  transfers between devices with their start and end apart: 9, of which 4 were waited for; matrix products, arithmetic and copies ran while one was open for 4% of the time, Pallas kernels for 0%

profile of v1, /device:TPU:1, one launch (start us, length us, event | category | flops | bytes accessed | tf_op | source)
XLA Modules:
  0.0 1491.5 jit_solution(10087968989301413361)
XLA Ops:
  0.0 28.4 %all_gather.3 = bf16[3,128,1024]{2,1,0:T(8,128)(2,1)S(1)} all-gather(bf16[3,16,1024]{2,1,0:T(8,128)(2,1)} %param.9), channel_id=1, replica_groups=mesh['mesh'=4,'mode'=8] {'mode'}, dimensions={1}, use_global_device_ids=true | all-gather | bytes 884736 | tf_op jit(solution)/shard_map/all_gather | solution.py:78
  28.4 0.7 copy.37
  29.1 0.0 slice-start.8
  29.1 0.0 slice-start.9
  29.1 16.5 %copy.64 = bf16[32,128,1024]{2,0,1:T(8,128)(2,1)S(1)} copy(f32[32,128,1024]{2,1,0:T(8,128)} %param.8) | data formatting | bytes 25165824 | tf_op args[0]
  45.6 0.0 copy-start.1
  45.6 0.0 slice-start.11
  45.7 8.0 collective-permute-start.1
  53.7 3.7 collective-permute-start
  57.4 11.4 copy.66
  68.8 11.4 copy.46
  80.2 14.2 fusion.11
  94.5 51.6 %fusion.6 = (f32[32,128,1024]{2,0,1:T(8,128)}, f32[32,128,1024]{2,0,1:T(8,128)}, f32[32,128,1024]{2,0,1:T(8,128)}, f32[32,128,1024]{2,0,1:T(8,128)}) fusion(f32[1,32,130,1026]{3,1,2,0:T(8,128)} %fusion.11), kind=kLoop, calls=%fused_computation.19 | loop fusion | flops 16777216 | bytes 150994944 | tf_op jit(solution)/shard_map/mul | solution.py:58
  146.1 17.7 %copy.45 = f32[32,128,1024]{2,1,0:T(8,128)} copy(f32[32,128,1024]{2,0,1:T(8,128)} %get-tuple-element.17) | data formatting | bytes 33554432 | tf_op jit(solution)/shard_map/mul | solution.py:58
  163.7 2.8 fusion.38
  166.6 4.5 fusion.36
  171.1 0.9 copy.44
  172.0 0.0 slice-start.4
  172.1 0.0 slice-start.6
  172.1 0.0 slice-start.7
  172.1 21.0 %copy.43 = f32[32,128,1024]{2,1,0:T(8,128)} copy(f32[32,128,1024]{2,0,1:T(8,128)} %get-tuple-element.15) | data formatting | bytes 33554432 | tf_op jit(solution)/shard_map/mul | solution.py:58
  193.0 2.1 copy.42
  195.2 19.1 %copy.41 = f32[32,128,1024]{2,1,0:T(8,128)} copy(f32[32,128,1024]{2,0,1:T(8,128)S(1)} %bitcast.104) | data formatting | bytes 33554432 | tf_op jit(solution)/shard_map/mul | solution.py:58
  214.2 2.0 copy.40
  216.3 0.0 copy-start.2
  216.3 19.3 %copy.39 = f32[32,128,1024]{2,1,0:T(8,128)} copy(f32[32,128,1024]{2,0,1:T(8,128)S(1)} %bitcast.102) | data formatting | bytes 33554432 | tf_op jit(solution)/shard_map/mul | solution.py:58
  235.6 0.9 copy.38
  236.6 31.3 %add_convert_fusion = bf16[3,32,128,1024]{3,2,1,0:T(8,128)(2,1)} fusion(f32[32,128,1024]{2,1,0:T(8,128)S(1)} %bitcast.108, f32[3,128,1024]{2,1,0:T(8,128)S(1)} %copy.44, f32[32,128,1024]{2,1,0:T(8,128)} %copy.43, f32[3,128,1024]{2,1,0:T(8,128)S(1)} %copy-done.2, f32[32,128,1024]{2,1,0:T(8,128)} %copy.41, f32[3,128,1024]{2,1,0:T(8,128)} %copy.40, ...), kind=kLoop, calls=%fused_computation.3 | loop fusion | flops 100663296 | bytes 98566144 | tf_op jit(solution)/shard_map/convert_element_type | solution.py:59
  267.9 23.1 %pad_maximum_fusion = bf16[4,32,128,1024]{3,2,1,0:T(8,128)(2,1)} fusion(bf16[3,32,128,1024]{3,2,1,0:T(8,128)(2,1)} %add_convert_fusion, bf16[1,32,128,1024]{3,2,1,0:T(8,128)(2,1)} %copy.46), kind=kLoop, calls=%fused_computation.4 | loop fusion | flops 16777216 | bytes 67108864 | tf_op jit(solution)/shard_map/concatenate | solution.py:82
  291.0 20.6 %dynamic-slice_bitcast_fusion = (bf16[128,16,1024]{2,1,0:T(8,128)(2,1)}, bf16[128,16,1024]{2,1,0:T(8,128)(2,1)}, bf16[128,16,1024]{2,1,0:T(8,128)(2,1)}, bf16[12...) fusion(bf16[128,8,16,1024]{3,2,1,0:T(8,128)(2,1)} %bitcast.99, ...), kind=kLoop, calls=%fused_computation.43 | loop fusion | bytes 58720284 | tf_op jit(solution)/shard_map/squeeze | solution.py:24
  311.6 1.3 collective-permute-start.2
  312.9 0.9 collective-permute-start.4
  313.8 2.5 collective-permute-start.5
  316.2 3.2 collective-permute-start.6
  319.5 87.7 %collective-permute-done.2 = bf16[128,16,1024]{2,1,0:T(8,128)(2,1)} collective-permute-done((bf16[128,16,1024]{2,1,0:T(8,128)(2,1)}, bf16[128,16,1024]{2,1,0:T(8,128)(2,1)}, u32[]{:S(2)}, u32[]{:S(2)}) %collective-permute-start.2) | collective-permute-done | bytes 4194336 | tf_op jit(solution)/shard_map/ppermute | solution.py:25
  407.2 0.5 collective-permute-done.3
  407.7 89.8 %collective-permute-start.8 = (bf16[128,16,1024]{2,1,0:T(8,128)(2,1)}, bf16[128,16,1024]{2,1,0:T(8,128)(2,1)}, u32[]{:S(2)}, u32[]{:S(2)}) collective-permute-start(bf16[128,16,1024]{2,1,0:T(8,128)(2,1)} %get-tuple-element.7), channel_id=1, source_target_pairs={{0,7},{1,0},{2,1},{3,2},{4,3},{5,4},{6,5},{7,6},{8,15},{9,8},{10,9... | collective-permute-start | bytes 12582920 | tf_op jit(solution)/shard_map/ppermute | solution.py:25
  497.5 5.1 bitcast_dynamic-update-slice_fusion.7
  502.6 5.0 bitcast_dynamic-update-slice_fusion.6
  507.6 5.0 bitcast_dynamic-update-slice_fusion.5
  512.7 253.9 %collective-permute-done.4 = bf16[128,16,1024]{2,1,0:T(8,128)(2,1)} collective-permute-done((bf16[128,16,1024]{2,1,0:T(8,128)(2,1)}, bf16[128,16,1024]{2,1,0:T(8,128)(2,1)}, u32[]{:S(2)}, u32[]{:S(2)}) %collective-permute-start.4) | collective-permute-done | bytes 4194336 | tf_op jit(solution)/shard_map/ppermute | solution.py:25
  766.5 5.0 bitcast_dynamic-update-slice_fusion.4
  771.5 5.1 bitcast_dynamic-update-slice_fusion.3
  776.7 5.0 bitcast_dynamic-update-slice_fusion.2
  781.7 5.0 bitcast_dynamic-update-slice_fusion.1
  786.7 66.1 %collective-permute-done.8 = bf16[128,16,1024]{2,1,0:T(8,128)(2,1)} collective-permute-done((bf16[128,16,1024]{2,1,0:T(8,128)(2,1)}, bf16[128,16,1024]{2,1,0:T(8,128)(2,1)}, u32[]{:S(2)}, u32[]{:S(2)}) %collective-permute-start.8) | collective-permute-done | bytes 4194336 | tf_op jit(solution)/shard_map/ppermute | solution.py:25
  852.8 5.0 bitcast_dynamic-update-slice_fusion
  857.8 7.3 mini-gather-slice.5
  865.1 18.3 %fusion.50 = (bf16[8,128,16,384]{3,2,1,0:T(8,128)(2,1)}, bf16[8,128,16,384]{3,2,1,0:T(8,128)(2,1)}) fusion(bf16[8,128,16,1024]{3,2,1,0:T(8,128)(2,1)} %bitcast_dynamic-update-slice_fusion), kind=kLoop, calls=%fused_computation.86 | loop fusion | bytes 50331648 | tf_op jit(solution)/shard_map/gather | solution.py:26
  883.4 8.1 gather_fusion.2
  891.5 11.4 gather_fusion.1
  902.9 11.4 gather_fusion
  914.3 22.8 %pad_maximum_fusion.1 = bf16[8,128,16,1024]{3,2,1,0:T(8,128)(2,1)} fusion(bf16[8,128,16,256]{3,2,1,0:T(8,128)(2,1)} %gather_fusion.2, bf16[8,128,16,384]{3,2,1,0:T(8,128)(2,1)} %gather_fusion.1, bf16[8,128,16,384]{3,2,1,0:T(8,128)(2,1)} %gather_fusion), kind=kLoop, calls=%fused_computation.5 | loop fusion | flops 100663296 | bytes 67108864
  937.1 21.3 %slice.86 = bf16[3,8,32,16,1024]{4,3,2,0,1:T(8,128)(2,1)} slice(bf16[4,8,32,16,1024]{4,3,2,0,1:T(8,128)(2,1)} %bitcast.97), slice={[1:4], [0:8], [0:32], [0:16], [0:1024]} | slice | bytes 50331648 | tf_op jit(solution)/shard_map/slice | solution.py:91
  958.4 8.7 slice.85
  967.1 21.4 %copy.48 = bf16[3,8,32,16,1024]{4,3,2,1,0:T(8,128)(2,1)} copy(bf16[3,8,32,16,1024]{4,3,2,0,1:T(8,128)(2,1)} %slice.86) | data formatting | bytes 50331648 | tf_op jit(solution)/shard_map/slice | solution.py:91
  988.5 0.0 copy-start.5
  988.5 0.0 copy-start.6
  988.5 0.0 copy-start.7
  988.5 77.9 %fusion = f32[16,1024,256,1]{2,1,3,0:T(8,128)} fusion(bf16[3,256,16,1024]{3,2,1,0:T(8,128)(2,1)} %bitcast.111, bf16[3,256,256]{2,1,0:T(8,128)(2,1)S(1)} %copy-done), kind=kOutput, calls=%fused_computation.9 | convolution fusion | flops 6442450944 | bytes 42336256 | tf_op jit(solution)/shard_map/kij,kjxy->ixy/dot_general | solution.py:63
  1066.4 22.8 %fusion.23 = bf16[256,16,1024]{0,2,1:T(8,128)(2,1)} fusion(f32[16,1024,256,1]{2,1,3,0:T(8,128)} %fusion, f32[512]{0:T(512)S(1)} %copy-done.6, f32[512]{0:T(512)S(1)} %copy-done.7, bf16[256,16,1024]{2,1,0:T(8,128)(2,1)} %bitcast.112, f32[16,1024]{1,0:T(8,128)S(1)} %copy-done.5, bf16[256,512]{1,0:T(8,128)(2,1)S(1)} %copy-done.3, ...), kind=kOutput, calls=%fused_computation.34 | convolution fusion | flops 8669626368 | bytes 34148352 | tf_op jit(solution)/shard_map/iq,qxy->ixy/dot_general | solution.py:68
  1089.2 12.2 copy.50
  1101.5 380.9 %all_to_all.18 = bf16[256,16,1024]{2,1,0:T(8,128)(2,1)} all-to-all(bf16[256,16,1024]{2,1,0:T(8,128)(2,1)} %copy.50), channel_id=1, replica_groups=mesh['mesh'=4,'mode'=8] {'mode'}, dimensions={0} | all-to-all | bytes 16777216 | tf_op jit(solution)/shard_map/all_to_all | solution.py:95
  1482.4 8.7 copy.51
  (51 shorter events, 0.1 us)
Async XLA Ops:
  0.0 988.4 %copy-start = (bf16[3,256,256]{2,1,0:T(8,128)(2,1)S(1)}, bf16[3,256,256]{2,1,0:T(8,128)(2,1)}, u32[]{:S(2)}) copy-start(bf16[3,256,256]{2,1,0:T(8,128)(2,1)} %param.11) | copy-start | bytes 1179652
  29.1 28.3 %slice-start.8 = ((s8[16777216]{0:T(1024)(128)(4,1)}), s8[4194304]{0:T(1024)(128)(4,1)S(1)}, s32[]{:S(2)}) async-start(s8[16777216]{0:T(1024)(128)(4,1)} %bitcast.105), calls=%async_computation.9 | async-start | bytes 8388608
  29.1 28.3 %slice-start.9 = ((s8[16777216]{0:T(1024)(128)(4,1)}), s8[4194304]{0:T(1024)(128)(4,1)S(1)}, s32[]{:S(2)}) async-start(s8[16777216]{0:T(1024)(128)(4,1)} %bitcast.105), calls=%async_computation.10 | async-start | bytes 8388608
  29.1 28.3 %slice-start.10 = ((s8[16777216]{0:T(1024)(128)(4,1)}), s8[4194304]{0:T(1024)(128)(4,1)S(1)}, s32[]{:S(2)}) async-start(s8[16777216]{0:T(1024)(128)(4,1)} %bitcast.105), calls=%async_computation.11 | async-start | bytes 8388608
  45.6 23.2 %copy-start.1 = (bf16[32,128,1024]{2,0,1:T(8,128)(2,1)}, bf16[32,128,1024]{2,0,1:T(8,128)(2,1)S(1)}, u32[]{:S(2)}) copy-start(bf16[32,128,1024]{2,0,1:T(8,128)(2,1)S(1)} %copy.64) | copy-start | bytes 25165828
  45.6 11.7 slice-start.11
  45.7 34.6 %collective-permute-start.1 = (bf16[35,1,1024]{2,0,1:T(8,128)(2,1)S(1)}, bf16[35,1,1024]{2,0,1:T(8,128)(2,1)S(1)}, u32[]{:S(2)}, u32[]{:S(2)}) collective-permute-start(bf16[35,1,1024]{2,0,1:T(8,128)(2,1)S(1)} %get-tuple-element.19), channel_id=1, source_target_pairs={{8,0},{16,8},{24,16},{9,1},{17,9},{25,17},{10,2},{18,10},{26,18},{... | collective-permute-start | bytes 215048 | tf_op jit(solution)/shard_map/ppermute | solution.py:40
  53.7 26.6 %collective-permute-start = (bf16[35,1,1024]{2,0,1:T(8,128)(2,1)S(1)}, bf16[35,1,1024]{2,0,1:T(8,128)(2,1)S(1)}, u32[]{:S(2)}, u32[]{:S(2)}) collective-permute-start(bf16[35,1,1024]{2,0,1:T(8,128)(2,1)S(1)} %get-tuple-element.18), channel_id=1, source_target_pairs={{0,8},{8,16},{16,24},{1,9},{9,17},{17,25},{2,10},{10,18},{18,26},{... | collective-permute-start | bytes 215048 | tf_op jit(solution)/shard_map/ppermute | solution.py:38
  172.0 23.1 %slice-start.4 = ((s8[16777216]{0:T(1024)(128)(4,1)}), s8[4194304]{0:T(1024)(128)(4,1)S(1)}, s32[]{:S(2)}) async-start(s8[16777216]{0:T(1024)(128)(4,1)} %bitcast.103), calls=%async_computation.5 | async-start | bytes 8388608
  172.1 23.1 %slice-start.5 = ((s8[16777216]{0:T(1024)(128)(4,1)}), s8[4194304]{0:T(1024)(128)(4,1)S(1)}, s32[]{:S(2)}) async-start(s8[16777216]{0:T(1024)(128)(4,1)} %bitcast.103), calls=%async_computation.6 | async-start | bytes 8388608
  172.1 23.0 %slice-start.6 = ((s8[16777216]{0:T(1024)(128)(4,1)}), s8[4194304]{0:T(1024)(128)(4,1)S(1)}, s32[]{:S(2)}) async-start(s8[16777216]{0:T(1024)(128)(4,1)} %bitcast.103), calls=%async_computation.7 | async-start | bytes 8388608
  172.1 23.0 %slice-start.7 = ((s8[16777216]{0:T(1024)(128)(4,1)}), s8[4194304]{0:T(1024)(128)(4,1)S(1)}, s32[]{:S(2)}) async-start(s8[16777216]{0:T(1024)(128)(4,1)} %bitcast.103), calls=%async_computation.8 | async-start | bytes 8388608
  195.1 21.2 %slice-start = ((s8[16777216]{0:T(1024)(128)(4,1)}), s8[4194304]{0:T(1024)(128)(4,1)S(1)}, s32[]{:S(2)}) async-start(s8[16777216]{0:T(1024)(128)(4,1)} %bitcast.101), calls=%async_computation.1 | async-start | bytes 8388608
  195.1 21.1 %slice-start.1 = ((s8[16777216]{0:T(1024)(128)(4,1)}), s8[4194304]{0:T(1024)(128)(4,1)S(1)}, s32[]{:S(2)}) async-start(s8[16777216]{0:T(1024)(128)(4,1)} %bitcast.101), calls=%async_computation.2 | async-start | bytes 8388608
  195.1 21.1 %slice-start.2 = ((s8[16777216]{0:T(1024)(128)(4,1)}), s8[4194304]{0:T(1024)(128)(4,1)S(1)}, s32[]{:S(2)}) async-start(s8[16777216]{0:T(1024)(128)(4,1)} %bitcast.101), calls=%async_computation.3 | async-start | bytes 8388608
  195.2 21.1 %slice-start.3 = ((s8[16777216]{0:T(1024)(128)(4,1)}), s8[4194304]{0:T(1024)(128)(4,1)S(1)}, s32[]{:S(2)}) async-start(s8[16777216]{0:T(1024)(128)(4,1)} %bitcast.101), calls=%async_computation.4 | async-start | bytes 8388608
  216.3 20.2 %slice-start.12 = ((s8[16777216]{0:T(1024)(128)(4,1)}), s8[4194304]{0:T(1024)(128)(4,1)S(1)}, s32[]{:S(2)}) async-start(s8[16777216]{0:T(1024)(128)(4,1)} %bitcast.107), calls=%async_computation.13 | async-start | bytes 8388608
  216.3 20.2 %slice-start.13 = ((s8[16777216]{0:T(1024)(128)(4,1)}), s8[4194304]{0:T(1024)(128)(4,1)S(1)}, s32[]{:S(2)}) async-start(s8[16777216]{0:T(1024)(128)(4,1)} %bitcast.107), calls=%async_computation.14 | async-start | bytes 8388608
  216.3 20.2 %slice-start.14 = ((s8[16777216]{0:T(1024)(128)(4,1)}), s8[4194304]{0:T(1024)(128)(4,1)S(1)}, s32[]{:S(2)}) async-start(s8[16777216]{0:T(1024)(128)(4,1)} %bitcast.107), calls=%async_computation.15 | async-start | bytes 8388608
  216.3 20.2 %slice-start.15 = ((s8[16777216]{0:T(1024)(128)(4,1)}), s8[4194304]{0:T(1024)(128)(4,1)S(1)}, s32[]{:S(2)}) async-start(s8[16777216]{0:T(1024)(128)(4,1)} %bitcast.107), calls=%async_computation.16 | async-start | bytes 8388608
  216.3 20.2 %copy-start.2 = (f32[3,128,1024]{2,1,0:T(8,128)S(1)}, f32[3,128,1024]{2,1,0:T(8,128)}, u32[]{:S(2)}) copy-start(f32[3,128,1024]{2,1,0:T(8,128)} %copy.42) | copy-start | bytes 4718596
  311.6 95.5 %collective-permute-start.2 = (bf16[128,16,1024]{2,1,0:T(8,128)(2,1)}, bf16[128,16,1024]{2,1,0:T(8,128)(2,1)}, u32[]{:S(2)}, u32[]{:S(2)}) collective-permute-start(bf16[128,16,1024]{2,1,0:T(8,128)(2,1)} %get-tuple-element.13), channel_id=1, source_target_pairs={{0,1},{1,2},{2,3},{3,4},{4,5},{5,6},{6,7},{7,0},{8,9},{9,10},{10,1... | collective-permute-start | bytes 12582920 | tf_op jit(solution)/shard_map/ppermute | solution.py:25
  312.9 94.7 %collective-permute-start.3 = (bf16[128,16,1024]{2,1,0:T(8,128)(2,1)}, bf16[128,16,1024]{2,1,0:T(8,128)(2,1)}, u32[]{:S(2)}, u32[]{:S(2)}) collective-permute-start(bf16[128,16,1024]{2,1,0:T(8,128)(2,1)} %get-tuple-element.12), channel_id=1, source_target_pairs={{0,2},{1,3},{2,4},{3,5},{4,6},{5,7},{6,0},{7,1},{8,10},{9,11},{10,... | collective-permute-start | bytes 12582920 | tf_op jit(solution)/shard_map/ppermute | solution.py:25
  312.9 453.6 %collective-permute-start.4 = (bf16[128,16,1024]{2,1,0:T(8,128)(2,1)}, bf16[128,16,1024]{2,1,0:T(8,128)(2,1)}, u32[]{:S(2)}, u32[]{:S(2)}) collective-permute-start(bf16[128,16,1024]{2,1,0:T(8,128)(2,1)} %get-tuple-element.11), channel_id=1, source_target_pairs={{0,3},{1,4},{2,5},{3,6},{4,7},{5,0},{6,1},{7,2},{8,11},{9,12},{10,... | collective-permute-start | bytes 12582920 | tf_op jit(solution)/shard_map/ppermute | solution.py:25
  313.8 457.8 %collective-permute-start.5 = (bf16[128,16,1024]{2,1,0:T(8,128)(2,1)}, bf16[128,16,1024]{2,1,0:T(8,128)(2,1)}, u32[]{:S(2)}, u32[]{:S(2)}) collective-permute-start(bf16[128,16,1024]{2,1,0:T(8,128)(2,1)} %get-tuple-element.10), channel_id=1, source_target_pairs={{0,4},{1,5},{2,6},{3,7},{4,0},{5,1},{6,2},{7,3},{8,12},{9,13},{10,... | collective-permute-start | bytes 12582920 | tf_op jit(solution)/shard_map/ppermute | solution.py:25
  316.2 460.4 %collective-permute-start.6 = (bf16[128,16,1024]{2,1,0:T(8,128)(2,1)}, bf16[128,16,1024]{2,1,0:T(8,128)(2,1)}, u32[]{:S(2)}, u32[]{:S(2)}) collective-permute-start(bf16[128,16,1024]{2,1,0:T(8,128)(2,1)} %get-tuple-element.9), channel_id=1, source_target_pairs={{0,5},{1,6},{2,7},{3,0},{4,1},{5,2},{6,3},{7,4},{8,13},{9,14},{10,... | collective-permute-start | bytes 12582920 | tf_op jit(solution)/shard_map/ppermute | solution.py:25
  407.2 374.5 %collective-permute-start.7 = (bf16[128,16,1024]{2,1,0:T(8,128)(2,1)}, bf16[128,16,1024]{2,1,0:T(8,128)(2,1)}, u32[]{:S(2)}, u32[]{:S(2)}) collective-permute-start(bf16[128,16,1024]{2,1,0:T(8,128)(2,1)} %get-tuple-element.8), channel_id=1, source_target_pairs={{0,6},{1,7},{2,0},{3,1},{4,2},{5,3},{6,4},{7,5},{8,14},{9,15},{10,... | collective-permute-start | bytes 12582920 | tf_op jit(solution)/shard_map/ppermute | solution.py:25
  407.7 445.1 %collective-permute-start.8 = (bf16[128,16,1024]{2,1,0:T(8,128)(2,1)}, bf16[128,16,1024]{2,1,0:T(8,128)(2,1)}, u32[]{:S(2)}, u32[]{:S(2)}) collective-permute-start(bf16[128,16,1024]{2,1,0:T(8,128)(2,1)} %get-tuple-element.7), channel_id=1, source_target_pairs={{0,7},{1,0},{2,1},{3,2},{4,3},{5,4},{6,5},{7,6},{8,15},{9,8},{10,9... | collective-permute-start | bytes 12582920 | tf_op jit(solution)/shard_map/ppermute | solution.py:25
  988.4 77.9 %copy-start.3 = (bf16[256,512]{1,0:T(8,128)(2,1)S(1)}, bf16[256,512]{1,0:T(8,128)(2,1)}, u32[]{:S(2)}) copy-start(bf16[256,512]{1,0:T(8,128)(2,1)} %param.13) | copy-start | bytes 786436
  988.4 77.9 %copy-start.4 = (bf16[512,256]{1,0:T(8,128)(2,1)S(1)}, bf16[512,256]{1,0:T(8,128)(2,1)}, u32[]{:S(2)}) copy-start(bf16[512,256]{1,0:T(8,128)(2,1)} %param.12) | copy-start | bytes 786436
  988.5 78.0 %copy-start.5 = (f32[16,1024]{1,0:T(8,128)S(1)}, f32[16,1024]{1,0:T(8,128)}, u32[]{:S(2)}) copy-start(f32[16,1024]{1,0:T(8,128)} %param.10) | copy-start | bytes 196612
  988.5 78.0 %copy-start.6 = (f32[512]{0:T(512)S(1)}, f32[512]{0:T(512)}, u32[]{:S(2)}) copy-start(f32[512]{0:T(512)} %param.15) | copy-start | bytes 6148
  988.5 77.9 %copy-start.7 = (f32[512]{0:T(512)S(1)}, f32[512]{0:T(512)}, u32[]{:S(2)}) copy-start(f32[512]{0:T(512)} %param.14) | copy-start | bytes 6148
